TPU v7x, 32 devices: a whole 2x2x4 slice. The times are simulated.
32 devices in a mesh: seq: 4 (over y, core), mem: 8 (over z, x).
Axes of the slice: x: 2, y: 2, z: 4, core: 2. Of those that a mesh axis runs over, the one named last changes fastest.
Arguments:
- queries: bfloat16 [128, 64, 2048], P('mem', 'seq'), may hold values from -40 to 40
- keys: bfloat16 [32, 128, 2048], P('mem'), may hold values from -8 to 8
- values: bfloat16 [32, 128, 2048], P('mem'), may hold values from -6 to 6
- grad_out: bfloat16 [128, 64, 2048], P('mem', 'seq'), may hold values from -6 to 6
- neighbour_owner: int32 [128, 2], replicated, may hold values from 0 to 7, all different within a row; in each aligned block of 16 rows (0 to 15, 16 to 31, ...) at most 6 rows name the same one
- neighbour_row: int32 [128, 2], replicated, may hold values from 0 to 3
Outputs:
- attended: bfloat16 [128, 64, 2048], P('mem', 'seq')
- grad_queries: bfloat16 [128, 64, 2048], P('mem', 'seq')
- grad_keys: bfloat16 [32, 128, 2048], P('mem', 'seq')
- grad_values: bfloat16 [32, 128, 2048], P('mem', 'seq')
Inputs may be any that keep to these rules, and one draw needn't show every extreme that they name: `neighbour_owner`: A group's two entries lie on different shards. Among the 16 groups of one index of mem (aligned blocks of rows) at most 6 name one shard, and exactly 6 do for some shard.
All inputs are finite; a program needn't handle non-finite values.
Results may differ from a plain program's by a relative error of at most 0.015.
Values may be sent and summed in bfloat16 or wider, within the bound.
A program may use at most 128 MiB of HBM per device.

v0:
```python
import math
import jax
import jax.numpy as jnp
from jax import lax
from jax.sharding import PartitionSpec as P

HEADS = 16


def route_tables(owners, shard_cap):
    ref_count = owners.shape[1]
    same_owner = owners[:, :, None] == owners[:, None, :]
    earlier = jnp.arange(ref_count)[None, :] < jnp.arange(ref_count)[:, None]
    rank_table = jnp.sum(same_owner & earlier[None], axis=2)
    return (rank_table, owners * shard_cap + rank_table)


def place_rows(source, slot_table, slot_total):
    buffer = jnp.zeros((slot_total,) + source.shape[1:], source.dtype)
    return buffer.at[slot_table].set(source)


def per_device(queries, keys, values, grad_out, neighbour_owner, neighbour_row):
    senders = lax.axis_size("mem")
    my_index = lax.axis_index("mem")
    group_dev, token_piece, feature_count = queries.shape
    shard_rows, key_len, _ = keys.shape
    head_count = HEADS
    head_width = feature_count // head_count
    scaling = 1.0 / math.sqrt(head_width)
    ref_count = 2 * group_dev
    shard_cap = max(2, 3 * group_dev // senders)
    slot_total = senders * shard_cap
    row_total = slot_total * token_piece
    owners = neighbour_owner.reshape(senders, ref_count)
    row_ids = neighbour_row.reshape(senders, ref_count)
    rank_table, slot_all = route_tables(owners, shard_cap)
    my_slots = lax.dynamic_index_in_dim(slot_all, my_index, 0, keepdims=False)
    owner_hits = owners == my_index
    picked = owner_hits[:, :, None] & (
        rank_table[:, :, None] == jnp.arange(shard_cap)[None, None, :]
    )
    slot_valid = jnp.any(picked, axis=1).reshape(slot_total)
    slot_row = jnp.sum(jnp.where(picked, row_ids[:, :, None], 0), axis=1).reshape(slot_total)
    send_queries = place_rows(jnp.repeat(queries, 2, axis=0), my_slots, slot_total)
    send_grads = place_rows(jnp.repeat(grad_out, 2, axis=0), my_slots, slot_total)
    got_queries = lax.all_to_all(send_queries, "mem", split_axis=0, concat_axis=0, tiled=True)
    query_heads = jnp.moveaxis(got_queries.reshape(row_total, head_count, head_width), 1, 0)
    key_heads = jnp.moveaxis(keys.reshape(shard_rows * key_len, head_count, head_width), 1, 0)
    value_heads = jnp.moveaxis(values.reshape(shard_rows * key_len, head_count, head_width), 1, 0)
    row_owner = jnp.repeat(slot_row, token_piece)
    key_owner = jnp.repeat(jnp.arange(shard_rows, dtype=jnp.int32), key_len)
    own_keys = row_owner[:, None] == key_owner[None, :]

    def head_scores(query_one, key_one):
        return (
            jnp.einsum("td,kd->tk", query_one, key_one, preferred_element_type=jnp.float32)
            * scaling
        )

    def forward_head(operands):
        query_one, key_one, value_one = operands
        scores = head_scores(query_one, key_one)
        peak = jnp.max(jnp.where(own_keys, scores, -jnp.inf), axis=1)
        exponent = jnp.where(own_keys, jnp.exp(scores - peak[:, None]), 0.0).astype(jnp.bfloat16)
        norm = jnp.sum(exponent, axis=1, dtype=jnp.float32)
        mix = (
            jnp.einsum("tk,kd->td", exponent, value_one, preferred_element_type=jnp.float32)
            / norm[:, None]
        )
        return (mix, peak, norm)

    head_mix, row_peak, row_norm = lax.map(forward_head, (query_heads, key_heads, value_heads))
    partial_mix = jnp.moveaxis(head_mix, 0, 1)
    back_mix, back_peak, back_norm = (
        lax.all_to_all(
            partial_mix.reshape(slot_total, token_piece, feature_count),
            "mem",
            split_axis=0,
            concat_axis=0,
            tiled=True,
        ),
        lax.all_to_all(
            row_peak.T.reshape(slot_total, token_piece, head_count),
            "mem",
            split_axis=0,
            concat_axis=0,
            tiled=True,
        ),
        lax.all_to_all(
            row_norm.T.reshape(slot_total, token_piece, head_count),
            "mem",
            split_axis=0,
            concat_axis=0,
            tiled=True,
        ),
    )
    part_mix = jnp.take(back_mix, my_slots, axis=0).reshape(
        group_dev, 2, token_piece, head_count, head_width
    )
    part_peak = jnp.take(back_peak, my_slots, axis=0).reshape(group_dev, 2, token_piece, head_count)
    part_norm = jnp.take(back_norm, my_slots, axis=0).reshape(group_dev, 2, token_piece, head_count)
    row_top = jnp.max(part_peak, axis=1)
    weight = jnp.exp(part_peak - row_top[:, None]) * part_norm
    total_norm = jnp.sum(weight, axis=1)
    attended_heads = (jnp.sum(weight[..., None] * part_mix, axis=1) / total_norm[..., None]).astype(
        jnp.bfloat16
    )
    attended = attended_heads.reshape(group_dev, token_piece, feature_count)
    row_dsum = jnp.sum(
        grad_out.reshape(group_dev, token_piece, head_count, head_width).astype(jnp.float32)
        * attended_heads.astype(jnp.float32),
        axis=3,
    )
    send_top = place_rows(jnp.repeat(row_top, 2, axis=0), my_slots, slot_total)
    send_norm = place_rows(jnp.repeat(total_norm, 2, axis=0), my_slots, slot_total)
    send_dsum = place_rows(jnp.repeat(row_dsum, 2, axis=0), my_slots, slot_total)
    got_grads = lax.all_to_all(send_grads, "mem", split_axis=0, concat_axis=0, tiled=True)
    got_top, got_norm, got_dsum = (
        lax.all_to_all(send_top, "mem", split_axis=0, concat_axis=0, tiled=True),
        lax.all_to_all(send_norm, "mem", split_axis=0, concat_axis=0, tiled=True),
        lax.all_to_all(send_dsum, "mem", split_axis=0, concat_axis=0, tiled=True),
    )
    safe_norm = jnp.where(slot_valid[:, None, None], got_norm, 1.0)
    grad_heads = jnp.moveaxis(got_grads.reshape(row_total, head_count, head_width), 1, 0)
    stat_top = got_top.reshape(row_total, head_count).T
    stat_norm = safe_norm.reshape(row_total, head_count).T
    stat_dsum = got_dsum.reshape(row_total, head_count).T

    def backward_head(operands):
        query_one, key_one, value_one, grad_one, top_one, norm_one, dsum_one = operands
        scores = head_scores(query_one, key_one)
        probability = (
            jnp.where(own_keys, jnp.exp(scores - top_one[:, None]), 0.0) / norm_one[:, None]
        )
        prob_half = probability.astype(jnp.bfloat16)
        value_grad = jnp.einsum(
            "tk,td->kd", prob_half, grad_one, preferred_element_type=jnp.float32
        )
        prob_grad = jnp.einsum("td,kd->tk", grad_one, value_one, preferred_element_type=jnp.float32)
        score_half = (probability * (prob_grad - dsum_one[:, None]) * scaling).astype(jnp.bfloat16)
        query_part = jnp.einsum(
            "tk,kd->td", score_half, key_one, preferred_element_type=jnp.float32
        )
        key_grad = jnp.einsum(
            "tk,td->kd", score_half, query_one, preferred_element_type=jnp.float32
        )
        return (query_part, key_grad, value_grad)

    head_query, head_key, head_value = lax.map(
        backward_head,
        (query_heads, key_heads, value_heads, grad_heads, stat_top, stat_norm, stat_dsum),
    )
    query_parts = jnp.moveaxis(head_query, 0, 1)
    key_grads = jnp.moveaxis(head_key, 0, 1)
    value_grads = jnp.moveaxis(head_value, 0, 1)
    returned = lax.all_to_all(
        query_parts.reshape(slot_total, token_piece, feature_count),
        "mem",
        split_axis=0,
        concat_axis=0,
        tiled=True,
    )
    own_grads = jnp.take(returned, my_slots, axis=0).reshape(
        group_dev, 2, token_piece, feature_count
    )
    grad_queries = (own_grads[:, 0] + own_grads[:, 1]).astype(jnp.bfloat16)
    memory_sums = (
        lax.psum_scatter(
            key_grads.reshape(shard_rows, key_len, feature_count),
            "seq",
            scatter_dimension=1,
            tiled=True,
        ),
        lax.psum_scatter(
            value_grads.reshape(shard_rows, key_len, feature_count),
            "seq",
            scatter_dimension=1,
            tiled=True,
        ),
    )
    return (
        attended,
        grad_queries,
        memory_sums[0].astype(jnp.bfloat16),
        memory_sums[1].astype(jnp.bfloat16),
    )


def solution(mesh):
    placed = (
        P("mem", "seq", None),
        P("mem", None, None),
        P("mem", None, None),
        P("mem", "seq", None),
        P(),
        P(),
    )
    return jax.shard_map(
        per_device,
        mesh=mesh,
        in_specs=placed,
        out_specs=(
            P("mem", "seq", None),
            P("mem", "seq", None),
            P("mem", "seq", None),
            P("mem", "seq", None),
        ),
        check_vma=False,
    )
```

profile of v0, /device:TPU:0, one launch (start us, length us, event | category | flops | bytes accessed | tf_op | source)
XLA Modules:
  0.0 814.0 jit_solution(18318656970991013179)
XLA Ops:
  12.0 5.4 scatter_fusion
  17.4 7.4 all-to-all-start
  32.7 62.8 %all-to-all-done = bf16[48,16,2048]{2,1,0:T(8,128)(2,1)S(1)} async-done(((bf16[48,16,2048]{2,1,0:T(8,128)(2,1)}), bf16[48,16,2048]{2,1,0:T(8,128)(2,1)S(1)}, u32[]{:S(2)}, u32[]{:S(2)}) %all-to-all-start) | async-done | bytes 3145760 | tf_op jit(solution)/shard_map/all_to_all | solution.py:47
  102.4 66.3 %while.30 = (s32[]{:T(128)}, f32[16,768,128]{2,1,0:T(8,128)}, f32[16,768]{1,0:T(8,128)S(1)}, f32[16,768]{1,0:T(8,128)S(1)}, bf16[16,768,128]{2,1,0:T(8,128)(2,1)...) while((s32[]{:T(128)}, f32[16,768,128]{2,1,0:T(8,128)}, ...), condition=%wide.region_6.7_spmd.clone, body=%wide.region_3.0_spmd.clone.sunk | while | flops 206928384 | bytes 5628029 | solution.py:73
  174.2 5.8 all-to-all-done.2
  185.7 5.4 scatter_fusion.3
  191.8 6.0 all-to-all-start.6
  214.9 52.0 %all-to-all-done.6 = bf16[48,16,2048]{2,1,0:T(8,128)(2,1)S(1)} async-done(((bf16[48,16,2048]{2,1,0:T(8,128)(2,1)}), bf16[48,16,2048]{2,1,0:T(8,128)(2,1)S(1)}, u32[]{:S(2)}, u32[]{:S(2)}) %all-to-all-start.6) | async-done | bytes 3145760 | tf_op jit(solution)/shard_map/all_to_all | solution.py:118
  270.6 9.0 %copy.40 = f32[768,16,128]{2,1,0:T(8,128)} copy(f32[768,16,128]{2,0,1:T(8,128)} %bitcast.163) | data formatting | bytes 12582912 | tf_op jit(solution)/shard_map/transpose | solution.py:74
  279.6 7.1 reshape.183
  287.3 6.0 all-to-all-start.3
  306.0 125.2 %all-to-all-done.3 = f32[48,16,2048]{2,1,0:T(8,128)} async-done(((f32[48,16,2048]{2,1,0:T(8,128)}), f32[48,16,2048]{2,1,0:T(8,128)}, u32[]{:S(2)}, u32[]{:S(2)}) %all-to-all-start.3) | async-done | bytes 6291488 | tf_op jit(solution)/shard_map/all_to_all | solution.py:76
  435.1 5.7 gather_fusion.2
  452.3 5.9 all-to-all-start.7
  473.2 153.4 %while.31 = (s32[]{:T(128)}, f32[16,768,128]{2,1,0:T(8,128)}, f32[16,512,128]{2,1,0:T(8,128)}, f32[16,512,128]{2,1,0:T(8,128)}, bf16[16,768,128]{2,1,0:T(8,128)(...) while((s32[]{:T(128)}, f32[16,768,128]{2,1,0:T(8,128)}, ...), condition=%wide.region_17.20_spmd.clone, body=%wide.region_16.19_spmd.clone.sunk | while | flops 507248640 | bytes 9214101 | solution.py:150
  626.6 6.6 copy.51
  638.1 9.1 %copy.49 = f32[768,16,128]{2,1,0:T(8,128)} copy(f32[768,16,128]{2,0,1:T(8,128)} %bitcast.162) | data formatting | bytes 12582912 | tf_op jit(solution)/shard_map/transpose | solution.py:154
  647.2 7.4 reshape.193
  654.6 6.0 all-to-all-start.8
  660.8 6.6 copy.50
  674.8 9.1 %reduce-scatter.5.cloned.1.call-done = f32[4,32,2048]{2,1,0:T(8,128)} async-done(((f32[4,128,2048]{2,1,0:T(8,128)}), f32[4,32,2048]{2,1,0:T(8,128)}) %reduce-scatter.5.cloned.1.call-update) | async-done | bytes 1048592 | tf_op jit(solution)/shard_map/reduce_scatter | solution.py:175
  686.0 45.1 %reduce-scatter.3.cloned.1.call-done = f32[4,32,2048]{2,1,0:T(8,128)} async-done(((f32[4,128,2048]{2,1,0:T(8,128)}), f32[4,32,2048]{2,1,0:T(8,128)}) %reduce-scatter.3.cloned.1.call-update) | async-done | bytes 1048592 | tf_op jit(solution)/shard_map/reduce_scatter | solution.py:169
  733.2 64.2 %all-to-all-done.8 = f32[48,16,2048]{2,1,0:T(8,128)} async-done(((f32[48,16,2048]{2,1,0:T(8,128)}), f32[48,16,2048]{2,1,0:T(8,128)}, u32[]{:S(2)}, u32[]{:S(2)}) %all-to-all-start.8) | async-done | bytes 6291488 | tf_op jit(solution)/shard_map/all_to_all | solution.py:157
  797.5 5.8 gather_fusion.3
  (353 shorter events, 334.8 us)
Async XLA Ops:
  8.4 177.3 %copy-start.11 = (s32[32]{0:T(128)}, s32[32]{0:T(128)S(1)}, u32[]{:S(2)}) copy-start(s32[32]{0:T(128)S(1)} %fusion.47) | copy-start | bytes 388
  17.4 7.4 copy-start.15
  17.4 78.1 %all-to-all-start = ((bf16[48,16,2048]{2,1,0:T(8,128)(2,1)}), bf16[48,16,2048]{2,1,0:T(8,128)(2,1)S(1)}, u32[]{:S(2)}, u32[]{:S(2)}) async-start(bf16[48,16,2048]{2,1,0:T(8,128)(2,1)} %scatter_fusion), calls=%async_computation | async-start | bytes 6291456 | tf_op jit(solution)/shard_map/all_to_all | solution.py:47
  28.3 1.9 copy-start.3
  102.4 81.1 %copy-start.1 = (bf16[16,16,2048]{2,1,0:T(8,128)(2,1)S(1)}, bf16[16,16,2048]{2,1,0:T(8,128)(2,1)}, u32[]{:S(2)}) copy-start(bf16[16,16,2048]{2,1,0:T(8,128)(2,1)} %param.17) | copy-start | bytes 3145732
  169.6 10.4 %all-to-all-start.2 = ((f32[8,1,1536]{2,1,0:T(1,128)}), f32[8,1,1536]{2,1,0:T(1,128)S(1)}, u32[]{:S(2)}, u32[]{:S(2)}) async-start(f32[8,1,1536]{2,1,0:T(1,128)} %reshape.285), calls=%async_computation.2 | async-start | bytes 98304 | tf_op jit(solution)/shard_map/all_to_all | solution.py:90
  180.0 11.1 %all-to-all-start.1 = ((f32[8,1,1536]{2,1,0:T(1,128)}), f32[8,1,1536]{2,1,0:T(1,128)S(1)}, u32[]{:S(2)}, u32[]{:S(2)}) async-start(f32[8,1,1536]{2,1,0:T(1,128)} %reshape.287), calls=%async_computation.1 | async-start | bytes 98304 | tf_op jit(solution)/shard_map/all_to_all | solution.py:83
  191.8 75.1 %all-to-all-start.6 = ((bf16[48,16,2048]{2,1,0:T(8,128)(2,1)}), bf16[48,16,2048]{2,1,0:T(8,128)(2,1)S(1)}, u32[]{:S(2)}, u32[]{:S(2)}) async-start(bf16[48,16,2048]{2,1,0:T(8,128)(2,1)} %scatter_fusion.3), calls=%async_computation.6 | async-start | bytes 6291456 | tf_op jit(solution)/shard_map/all_to_all | solution.py:118
  208.5 2.6 copy-start.6
  210.3 0.8 copy-start.4
  266.9 19.7 %all-to-all-start.5 = ((f32[8,1,1536]{2,1,0:T(1,128)}), f32[8,1,1536]{2,1,0:T(1,128)S(1)}, u32[]{:S(2)}, u32[]{:S(2)}) async-start(f32[8,1,1536]{2,1,0:T(1,128)} %reshape.291), calls=%async_computation.5 | async-start | bytes 98304 | tf_op jit(solution)/shard_map/all_to_all | solution.py:121
  286.7 6.6 copy-start.14
  287.3 143.8 %all-to-all-start.3 = ((f32[48,16,2048]{2,1,0:T(8,128)}), f32[48,16,2048]{2,1,0:T(8,128)}, u32[]{:S(2)}, u32[]{:S(2)}) async-start(f32[48,16,2048]{2,1,0:T(8,128)} %reshape.183), calls=%async_computation.3 | async-start | bytes 12582912 | tf_op jit(solution)/shard_map/all_to_all | solution.py:76
  298.1 0.9 copy-start.7
  298.1 1.7 copy-start.12
  431.1 21.2 %all-to-all-start.4 = ((f32[8,1,1536]{2,1,0:T(1,128)}), f32[8,1,1536]{2,1,0:T(1,128)}, u32[]{:S(2)}, u32[]{:S(2)}) async-start(f32[8,1,1536]{2,1,0:T(1,128)} %reshape.289), calls=%async_computation.4 | async-start | bytes 98304 | tf_op jit(solution)/shard_map/all_to_all | solution.py:120
  443.5 1.0 copy-start.8
  444.4 1.6 copy-start
  444.5 1.6 copy-start.5
  452.3 13.7 %all-to-all-start.7 = ((f32[8,1,1536]{2,1,0:T(1,128)}), f32[8,1,1536]{2,1,0:T(1,128)}, u32[]{:S(2)}, u32[]{:S(2)}) async-start(f32[8,1,1536]{2,1,0:T(1,128)} %reshape.293), calls=%async_computation.7 | async-start | bytes 98304 | tf_op jit(solution)/shard_map/all_to_all | solution.py:122
  458.2 225.7 %reduce-scatter.5.cloned.1.call-start = ((), (), s32[]{:S(2)}) async-start(), calls=%async_computation.12 | async-start | bytes 5242880 | tf_op jit(solution)/shard_map/reduce_scatter | solution.py:175
  654.6 142.9 %all-to-all-start.8 = ((f32[48,16,2048]{2,1,0:T(8,128)}), f32[48,16,2048]{2,1,0:T(8,128)}, u32[]{:S(2)}, u32[]{:S(2)}) async-start(f32[48,16,2048]{2,1,0:T(8,128)} %reshape.193), calls=%async_computation.8 | async-start | bytes 12582912 | tf_op jit(solution)/shard_map/all_to_all | solution.py:157
  660.5 70.6 %reduce-scatter.3.cloned.1.call-start = ((), (), s32[]{:S(2)}) async-start(), calls=%async_computation.11 | async-start | bytes 5242880 | tf_op jit(solution)/shard_map/reduce_scatter | solution.py:169
  672.3 1.3 copy-start.2
  (3 other events, 1.8 us)
Sparse Core Ops, SparseCore 0:
  638.2 45.6 reduce-scatter.4
  686.6 44.4 reduce-scatter.2
where the time goes:
time: 821 us; the launch traced here: 814 us
  waiting for transfers between devices  364 us (44%)
  matrix products  186 us (23%)
  local copies, waits for them, and re-layouts  168 us (20%)
  starting transfers between devices  46.4 us (6%)
  other arithmetic  34.1 us (4%)
  between operations  14.4 us (2%)
    all_to_all x1, waiting for transfers between devices, per_device(): lax.all_to_all(partial_mix.reshape(slot_total, token_piece, feature_count...  125 us
    all_to_all x1, waiting for transfers between devices, per_device(): lax.all_to_all(query_parts.reshape(slot_total, token_piece, feature_count...  64.2 us
    all_to_all x1, waiting for transfers between devices, per_device(): lax.all_to_all(send_queries, 'mem', split_axis=0, concat_axis=0, tiled=True)  62.8 us
    all_to_all x1, waiting for transfers between devices, per_device(): lax.all_to_all(send_grads, 'mem', split_axis=0, concat_axis=0, tiled=True)  52 us
    dot_general x32, matrix products, head_scores(): jnp.einsum('td,kd->tk', query_one, key_one, preferred_element_type=jnp.fl...  47.2 us
    reduce_scatter x1, waiting for transfers between devices, per_device(): lax.psum_scatter(key_grads.reshape(shard_rows, key_len, feature_count), '...  45.1 us
    dot_general x16, matrix products, forward_head(): jnp.einsum('tk,kd->td', exponent, value_one, preferred_element_type=jnp.f...  35 us
    dot_general x16, matrix products, backward_head(): jnp.einsum('tk,td->kd', score_half, query_one, preferred_element_type=jnp...  32.7 us
  transfers between devices with their start and end apart: 11, of which 7 were waited for; matrix products, arithmetic and copies ran while one was open for 15% of the time, Pallas kernels for 0%

commit v1 on v0

--- a/solution.py
+++ b/solution.py
@@ -5,6 +5,23 @@
 from jax.sharding import PartitionSpec as P
 
 HEADS = 16
+
+
+def area_enter(shard_in, axis_id):
+    wide_out, y1 = (lax.axis_size(axis_id), lax.axis_index(axis_id))
+    vec_out = shard_in.shape[0] // wide_out
+    latest = jnp.roll(shard_in, -y1 * vec_out, axis=0)
+    entries = [lax.slice_in_dim(latest, 0, vec_out, axis=0)]
+    for tick in tuple(range(1, wide_out)):
+        o_now = lax.slice_in_dim(latest, tick * vec_out, (tick + 1) * vec_out, axis=0)
+        entries.append(
+            lax.ppermute(
+                o_now,
+                axis_id,
+                perm=[(hop_no, (hop_no + tick) % wide_out) for hop_no in range(wide_out)],
+            )
+        )
+    return jnp.roll(jnp.concatenate(entries[::-1], axis=0), (y1 + 1) * entries[0].shape[0], axis=0)
 
 
 def route_tables(owners, shard_cap):
@@ -154,13 +171,7 @@
     query_parts = jnp.moveaxis(head_query, 0, 1)
     key_grads = jnp.moveaxis(head_key, 0, 1)
     value_grads = jnp.moveaxis(head_value, 0, 1)
-    returned = lax.all_to_all(
-        query_parts.reshape(slot_total, token_piece, feature_count),
-        "mem",
-        split_axis=0,
-        concat_axis=0,
-        tiled=True,
-    )
+    returned = area_enter(query_parts.reshape(slot_total, token_piece, feature_count), "mem")
     own_grads = jnp.take(returned, my_slots, axis=0).reshape(
         group_dev, 2, token_piece, feature_count
     )

time: 821 us -> 895 us (1.090)
  local copies, waits for them, and re-layouts: 168 us -> 214 us
  waiting for transfers between devices: 364 us -> 375 us
    ppermute x0 -> x7, waiting for transfers between devices: none -> 128 us  [area_enter(): lax.ppermute(o_now, axis_id, perm=[(hop_no, (hop_no + tick) % wide_out) f...]
    all_to_all x1 -> x0, waiting for transfers between devices: 64.2 us -> none  [per_device(): lax.all_to_all(query_parts.reshape(slot_total, token_piece, feature_count...]
    reduce_scatter x1, waiting for transfers between devices: 45.1 us -> 0.01 us  [per_device(): lax.psum_scatter(key_grads.reshape(shard_rows, key_len, feature_count), '...]
    dynamic_update_slice x32, local copies, waits for them, and re-layouts: 2.8 us -> 43.6 us  [per_device(): lax.map(forward_head, (query_heads, key_heads, value_heads))]
    concatenate x0 -> x2, other arithmetic: none -> 9.64 us  [the longest x1 4.97 us: area_enter(): jnp.roll(jnp.concatenate(entries[::-1], axis=0), (y1 + 1) * entries[0].sh...]
    reduce_scatter x1, waiting for transfers between devices: 9.08 us -> 0.01 us  [per_device(): lax.psum_scatter(value_grads.reshape(shard_rows, key_len, feature_count),...]
    unnamed x54 -> x65, local copies, waits for them, and re-layouts: 29.4 us -> 28.6 us
  transfers between devices with their start and end apart: 11 -> 17, of which waited for: 7 -> 10; matrix products, arithmetic and copies ran while one was open for 15% -> 16% of each run, Pallas kernels for 0% -> 0%
where the time goes in v1:
time: 895 us; the launch traced here: 879 us
  waiting for transfers between devices  375 us (42%)
  local copies, waits for them, and re-layouts  214 us (24%)
  matrix products  184 us (21%)
  starting transfers between devices  48.5 us (5%)
  other arithmetic  41.6 us (5%)
  between operations  15.1 us (2%)
    ppermute x7, waiting for transfers between devices, area_enter(): lax.ppermute(o_now, axis_id, perm=[(hop_no, (hop_no + tick) % wide_out) f...  128 us
    all_to_all x1, waiting for transfers between devices, per_device(): lax.all_to_all(partial_mix.reshape(slot_total, token_piece, feature_count...  125 us
    all_to_all x1, waiting for transfers between devices, per_device(): lax.all_to_all(send_queries, 'mem', split_axis=0, concat_axis=0, tiled=True)  62.7 us
    all_to_all x1, waiting for transfers between devices, per_device(): lax.all_to_all(send_grads, 'mem', split_axis=0, concat_axis=0, tiled=True)  53.2 us
    dot_general x32, matrix products, head_scores(): jnp.einsum('td,kd->tk', query_one, key_one, preferred_element_type=jnp.fl...  45.7 us
    dynamic_update_slice x32, local copies, waits for them, and re-layouts, per_device(): lax.map(forward_head, (query_heads, key_heads, value_heads))  43.6 us
    dot_general x16, matrix products, forward_head(): jnp.einsum('tk,kd->td', exponent, value_one, preferred_element_type=jnp.f...  35 us
    dot_general x16, matrix products, backward_head(): jnp.einsum('tk,td->kd', score_half, query_one, preferred_element_type=jnp...  32.6 us
  transfers between devices with their start and end apart: 17, of which 10 were waited for; matrix products, arithmetic and copies ran while one was open for 16% of the time, Pallas kernels for 0%

profile of v1, /device:TPU:0, one launch (start us, length us, event | category | flops | bytes accessed | tf_op | source)
XLA Modules:
  0.0 879.2 jit_solution(9280698889937461215)
XLA Ops:
  12.0 5.4 scatter_fusion
  17.4 7.4 all-to-all-start
  32.7 62.7 %all-to-all-done = bf16[48,16,2048]{2,1,0:T(8,128)(2,1)S(1)} async-done(((bf16[48,16,2048]{2,1,0:T(8,128)(2,1)}), bf16[48,16,2048]{2,1,0:T(8,128)(2,1)S(1)}, u32[]{:S(2)}, u32[]{:S(2)}) %all-to-all-start) | async-done | bytes 3145760 | tf_op jit(solution)/shard_map/all_to_all | solution.py:64
  100.6 105.0 %while.30 = (s32[]{:T(128)}, f32[16,768,128]{2,1,0:T(8,128)}, f32[16,768]{1,0:T(8,128)}, f32[16,768]{1,0:T(8,128)}, bf16[16,768,128]{2,1,0:T(8,128)(2,1)S(1)}, /...) while((s32[]{:T(128)}, f32[16,768,128]{2,1,0:T(8,128)}, ...), condition=%wide.region_6.7_spmd.clone, body=%wide.region_3.0_spmd.clone.sunk | while | flops 206928384 | bytes 5629045 | solution.py:90
  225.1 5.4 scatter_fusion.3
  230.5 6.0 all-to-all-start.6
  252.2 53.2 %all-to-all-done.6 = bf16[48,16,2048]{2,1,0:T(8,128)(2,1)S(1)} async-done(((bf16[48,16,2048]{2,1,0:T(8,128)(2,1)}), bf16[48,16,2048]{2,1,0:T(8,128)(2,1)S(1)}, u32[]{:S(2)}, u32[]{:S(2)}) %all-to-all-start.6) | async-done | bytes 3145760 | tf_op jit(solution)/shard_map/all_to_all | solution.py:135
  309.2 9.1 %copy.40 = f32[768,16,128]{2,1,0:T(8,128)} copy(f32[768,16,128]{2,0,1:T(8,128)} %bitcast.158) | data formatting | bytes 12582912 | tf_op jit(solution)/shard_map/transpose | solution.py:91
  318.3 7.1 reshape.183
  326.0 6.0 all-to-all-start.3
  344.7 125.2 %all-to-all-done.3 = f32[48,16,2048]{2,1,0:T(8,128)} async-done(((f32[48,16,2048]{2,1,0:T(8,128)}), f32[48,16,2048]{2,1,0:T(8,128)}, u32[]{:S(2)}, u32[]{:S(2)}) %all-to-all-start.3) | async-done | bytes 6291488 | tf_op jit(solution)/shard_map/all_to_all | solution.py:93
  473.8 5.8 gather_fusion.2
  491.0 5.9 all-to-all-start.7
  511.0 153.4 %while.31 = (s32[]{:T(128)}, f32[16,768,128]{2,1,0:T(8,128)}, f32[16,512,128]{2,1,0:T(8,128)}, f32[16,512,128]{2,1,0:T(8,128)}, bf16[16,768,128]{2,1,0:T(8,128)(...) while((s32[]{:T(128)}, f32[16,768,128]{2,1,0:T(8,128)}, ...), condition=%wide.region_17.20_spmd.clone, body=%wide.region_16.19_spmd.clone.sunk | while | flops 507248640 | bytes 9214093 | solution.py:167
  664.4 6.7 copy.50
  676.0 6.7 copy.51
  682.7 5.2 reshape.196
  688.0 9.1 %copy.49 = f32[768,16,128]{2,1,0:T(8,128)} copy(f32[768,16,128]{2,0,1:T(8,128)} %bitcast.157) | data formatting | bytes 12582912 | tf_op jit(solution)/shard_map/transpose | solution.py:171
  697.1 7.1 reshape.193
  722.0 13.6 %collective-permute-done = f32[6,16,2048]{2,1,0:T(8,128)} collective-permute-done((f32[6,16,2048]{2,1,0:T(8,128)}, f32[6,16,2048]{2,1,0:T(8,128)}, u32[]{:S(2)}, u32[]{:S(2)}) %collective-permute-start) | collective-permute-done | bytes 786464 | tf_op jit(solution)/shard_map/ppermute | solution.py:18
  736.8 15.7 %collective-permute-done.1 = f32[6,16,2048]{2,1,0:T(8,128)S(1)} collective-permute-done((f32[6,16,2048]{2,1,0:T(8,128)}, f32[6,16,2048]{2,1,0:T(8,128)S(1)}, u32[]{:S(2)}, u32[]{:S(2)}) %collective-permute-start.1) | collective-permute-done | bytes 786464 | tf_op jit(solution)/shard_map/ppermute | solution.py:18
  752.8 16.6 %collective-permute-done.2 = f32[6,16,2048]{2,1,0:T(8,128)S(1)} collective-permute-done((f32[6,16,2048]{2,1,0:T(8,128)}, f32[6,16,2048]{2,1,0:T(8,128)S(1)}, u32[]{:S(2)}, u32[]{:S(2)}) %collective-permute-start.2) | collective-permute-done | bytes 786464 | tf_op jit(solution)/shard_map/ppermute | solution.py:18
  769.5 82.0 %collective-permute-done.3 = f32[6,16,2048]{2,1,0:T(8,128)S(1)} collective-permute-done((f32[6,16,2048]{2,1,0:T(8,128)}, f32[6,16,2048]{2,1,0:T(8,128)S(1)}, u32[]{:S(2)}, u32[]{:S(2)}) %collective-permute-start.3) | collective-permute-done | bytes 786464 | tf_op jit(solution)/shard_map/ppermute | solution.py:18
  858.1 5.8 gather_fusion.3
  (380 shorter events, 396.0 us)
Async XLA Ops:
  8.4 3.6 copy-start.16
  8.4 216.7 %copy-start.11 = (s32[32]{0:T(128)}, s32[32]{0:T(128)S(1)}, u32[]{:S(2)}) copy-start(s32[32]{0:T(128)S(1)} %fusion.49) | copy-start | bytes 388
  17.4 7.4 copy-start.17
  17.4 78.1 %all-to-all-start = ((bf16[48,16,2048]{2,1,0:T(8,128)(2,1)}), bf16[48,16,2048]{2,1,0:T(8,128)(2,1)S(1)}, u32[]{:S(2)}, u32[]{:S(2)}) async-start(bf16[48,16,2048]{2,1,0:T(8,128)(2,1)} %scatter_fusion), calls=%async_computation | async-start | bytes 6291456 | tf_op jit(solution)/shard_map/all_to_all | solution.py:64
  205.6 12.6 %copy-start.2 = (bf16[16,768,128]{2,1,0:T(8,128)(2,1)}, bf16[16,768,128]{2,1,0:T(8,128)(2,1)S(1)}, u32[]{:S(2)}) copy-start(bf16[16,768,128]{2,1,0:T(8,128)(2,1)S(1)} %get-tuple-element.505) | copy-start | bytes 9437188
  207.4 10.8 %all-to-all-start.1 = ((f32[8,1,1536]{2,1,0:T(1,128)}), f32[8,1,1536]{2,1,0:T(1,128)}, u32[]{:S(2)}, u32[]{:S(2)}) async-start(f32[8,1,1536]{2,1,0:T(1,128)} %reshape.287), calls=%async_computation.1 | async-start | bytes 98304 | tf_op jit(solution)/shard_map/all_to_all | solution.py:100
  218.2 12.3 %all-to-all-start.2 = ((f32[8,1,1536]{2,1,0:T(1,128)}), f32[8,1,1536]{2,1,0:T(1,128)S(1)}, u32[]{:S(2)}, u32[]{:S(2)}) async-start(f32[8,1,1536]{2,1,0:T(1,128)} %reshape.285), calls=%async_computation.2 | async-start | bytes 98304 | tf_op jit(solution)/shard_map/all_to_all | solution.py:107
  230.5 74.9 %all-to-all-start.6 = ((bf16[48,16,2048]{2,1,0:T(8,128)(2,1)}), bf16[48,16,2048]{2,1,0:T(8,128)(2,1)S(1)}, u32[]{:S(2)}, u32[]{:S(2)}) async-start(bf16[48,16,2048]{2,1,0:T(8,128)(2,1)} %scatter_fusion.3), calls=%async_computation.6 | async-start | bytes 6291456 | tf_op jit(solution)/shard_map/all_to_all | solution.py:135
  237.1 11.2 %copy-start.13 = (s32[1024]{0:T(1024)}, s32[1024]{0:T(1024)S(1)}, u32[]{:S(2)}) copy-start(s32[1024]{0:T(1024)S(1)} %pad_clamp_fusion) | copy-start | bytes 12292
  305.4 20.0 %all-to-all-start.5 = ((f32[8,1,1536]{2,1,0:T(1,128)}), f32[8,1,1536]{2,1,0:T(1,128)S(1)}, u32[]{:S(2)}, u32[]{:S(2)}) async-start(f32[8,1,1536]{2,1,0:T(1,128)} %reshape.291), calls=%async_computation.5 | async-start | bytes 98304 | tf_op jit(solution)/shard_map/all_to_all | solution.py:138
  326.0 143.8 %all-to-all-start.3 = ((f32[48,16,2048]{2,1,0:T(8,128)}), f32[48,16,2048]{2,1,0:T(8,128)}, u32[]{:S(2)}, u32[]{:S(2)}) async-start(f32[48,16,2048]{2,1,0:T(8,128)} %reshape.183), calls=%async_computation.3 | async-start | bytes 12582912 | tf_op jit(solution)/shard_map/all_to_all | solution.py:93
  469.8 21.2 %all-to-all-start.4 = ((f32[8,1,1536]{2,1,0:T(1,128)}), f32[8,1,1536]{2,1,0:T(1,128)}, u32[]{:S(2)}, u32[]{:S(2)}) async-start(f32[8,1,1536]{2,1,0:T(1,128)} %reshape.289), calls=%async_computation.4 | async-start | bytes 98304 | tf_op jit(solution)/shard_map/all_to_all | solution.py:137
  491.0 12.8 %all-to-all-start.7 = ((f32[8,1,1536]{2,1,0:T(1,128)}), f32[8,1,1536]{2,1,0:T(1,128)}, u32[]{:S(2)}, u32[]{:S(2)}) async-start(f32[8,1,1536]{2,1,0:T(1,128)} %reshape.293), calls=%async_computation.7 | async-start | bytes 98304 | tf_op jit(solution)/shard_map/all_to_all | solution.py:139
  496.9 370.8 %reduce-scatter.3.cloned.1.call-start = ((), (), s32[]{:S(2)}) async-start(), calls=%async_computation.10 | async-start | bytes 5242880 | tf_op jit(solution)/shard_map/reduce_scatter | solution.py:180
  675.9 193.9 %reduce-scatter.5.cloned.1.call-start = ((), (), s32[]{:S(2)}) async-start(), calls=%async_computation.11 | async-start | bytes 5242880 | tf_op jit(solution)/shard_map/reduce_scatter | solution.py:186
  708.9 4.3 copy-start
  708.9 11.9 %copy-start.3 = (bf16[16,16,16,128]{3,2,1,0:T(8,128)(2,1)S(1)}, bf16[16,16,16,128]{3,2,1,0:T(8,128)(2,1)}, u32[]{:S(2)}) copy-start(bf16[16,16,16,128]{3,2,1,0:T(8,128)(2,1)} %get-tuple-element.262) | copy-start | bytes 3145732
  713.2 22.5 %collective-permute-start = (f32[6,16,2048]{2,1,0:T(8,128)}, f32[6,16,2048]{2,1,0:T(8,128)}, u32[]{:S(2)}, u32[]{:S(2)}) collective-permute-start(f32[6,16,2048]{2,1,0:T(8,128)} %get-tuple-element.277), channel_id=1, source_target_pairs={{0,7},{1,0},{2,1},{3,2},{4,3},{5,4},{6,5},{7,6},{8,15},{9,8},{10,9... | collective-permute-start | bytes 2359304 | tf_op jit(solution)/shard_map/ppermute | solution.py:18
  717.3 35.2 %collective-permute-start.1 = (f32[6,16,2048]{2,1,0:T(8,128)}, f32[6,16,2048]{2,1,0:T(8,128)S(1)}, u32[]{:S(2)}, u32[]{:S(2)}) collective-permute-start(f32[6,16,2048]{2,1,0:T(8,128)} %get-tuple-element.276), channel_id=1, source_target_pairs={{0,6},{1,7},{2,0},{3,1},{4,2},{5,3},{6,4},{7,5},{8,14},{9,15},{10,... | collective-permute-start | bytes 2359304 | tf_op jit(solution)/shard_map/ppermute | solution.py:18
  717.9 51.5 %collective-permute-start.2 = (f32[6,16,2048]{2,1,0:T(8,128)}, f32[6,16,2048]{2,1,0:T(8,128)S(1)}, u32[]{:S(2)}, u32[]{:S(2)}) collective-permute-start(f32[6,16,2048]{2,1,0:T(8,128)} %get-tuple-element.275), channel_id=1, source_target_pairs={{0,5},{1,6},{2,7},{3,0},{4,1},{5,2},{6,3},{7,4},{8,13},{9,14},{10,... | collective-permute-start | bytes 2359304 | tf_op jit(solution)/shard_map/ppermute | solution.py:18
  717.9 133.6 %collective-permute-start.3 = (f32[6,16,2048]{2,1,0:T(8,128)}, f32[6,16,2048]{2,1,0:T(8,128)S(1)}, u32[]{:S(2)}, u32[]{:S(2)}) collective-permute-start(f32[6,16,2048]{2,1,0:T(8,128)} %get-tuple-element.274), channel_id=1, source_target_pairs={{0,4},{1,5},{2,6},{3,7},{4,0},{5,1},{6,2},{7,3},{8,12},{9,13},{10,... | collective-permute-start | bytes 2359304 | tf_op jit(solution)/shard_map/ppermute | solution.py:18
  722.0 129.7 %collective-permute-start.4 = (f32[6,16,2048]{2,1,0:T(8,128)}, f32[6,16,2048]{2,1,0:T(8,128)S(1)}, u32[]{:S(2)}, u32[]{:S(2)}) collective-permute-start(f32[6,16,2048]{2,1,0:T(8,128)} %get-tuple-element.273), channel_id=1, source_target_pairs={{0,3},{1,4},{2,5},{3,6},{4,7},{5,0},{6,1},{7,2},{8,11},{9,12},{10,... | collective-permute-start | bytes 2359304 | tf_op jit(solution)/shard_map/ppermute | solution.py:18
  735.7 116.1 %collective-permute-start.5 = (f32[6,16,2048]{2,1,0:T(8,128)}, f32[6,16,2048]{2,1,0:T(8,128)S(1)}, u32[]{:S(2)}, u32[]{:S(2)}) collective-permute-start(f32[6,16,2048]{2,1,0:T(8,128)} %get-tuple-element.272), channel_id=1, source_target_pairs={{0,2},{1,3},{2,4},{3,5},{4,6},{5,7},{6,0},{7,1},{8,10},{9,11},{10,... | collective-permute-start | bytes 2359304 | tf_op jit(solution)/shard_map/ppermute | solution.py:18
  752.5 99.3 %collective-permute-start.6 = (f32[6,16,2048]{2,1,0:T(8,128)}, f32[6,16,2048]{2,1,0:T(8,128)S(1)}, u32[]{:S(2)}, u32[]{:S(2)}) collective-permute-start(f32[6,16,2048]{2,1,0:T(8,128)} %get-tuple-element.271), channel_id=1, source_target_pairs={{0,1},{1,2},{2,3},{3,4},{4,5},{5,6},{6,7},{7,0},{8,9},{9,10},{10,1... | collective-permute-start | bytes 2359304 | tf_op jit(solution)/shard_map/ppermute | solution.py:18
  (11 other events, 16.2 us)
Sparse Core Ops, SparseCore 0:
  676.1 45.0 reduce-scatter.2
  723.8 44.4 reduce-scatter.4
